TPU v7x, 512 devices: a whole 4x8x8 slice. The times are simulated.
512 devices in a mesh: batch: 64 (over z_lo, x, y), param: 8 (over z_hi, core).
Axes of the slice: x: 4, y: 8, z: 8 (z_hi: 4, z_lo: 2; z = z_hi * 2 + z_lo), core: 2. Of those that a mesh axis runs over, the one named last changes fastest.
Arguments:
- target_backbone_features: bfloat16 [4096, 2048], P(('batch', 'param')), may hold values from -6 to 6
- closing_layernorm_gain: float32 [2048], replicated, may hold values from 0.5 to 1.5
- projection_weights_table: bfloat16 [2048, 1024], P('batch', 'param'), may hold values from -0.125 to 0.125
- source_raw_vectors: bfloat16 [32768, 1024], P(('batch', 'param')), may hold values from -0.5 to 0.5
- matching_target_ids: int32 [32768], P(('batch', 'param')), may hold values from 0 to 4095
- sharpness_parameter: float32 [1], replicated, may hold values from 5 to 15
- similarity_shift_term: float32 [1], replicated, may hold values from -4 to -2
Outputs:
- state_grad: bfloat16 [32768, 1024], P(('batch', 'param'))
- head_grad: float32 [2048, 1024], P('batch', 'param')
All inputs are finite; a program needn't handle non-finite values.
Results may differ from a plain program's by a relative error of at most 0.02.
Values may be sent and summed in bfloat16 or wider, within the bound.
A program may use at most 64 MiB of HBM per device.

v0:
```python
import jax
import jax.numpy as jnp
from jax import lax
from jax.sharding import PartitionSpec as P


def body(
    target_backbone_features,
    closing_layernorm_gain,
    projection_weights_table,
    source_raw_vectors,
    matching_target_ids,
    sharpness_parameter,
    similarity_shift_term,
):
    param_count = lax.axis_size("param")
    goal_rows = target_backbone_features.shape[0]
    batch_count = lax.axis_size("batch")
    features = target_backbone_features.astype(jnp.float32)
    scaled = lax.rsqrt(jnp.mean(features * features, axis=1, keepdims=True) + 1e-06)
    normed = (features * scaled * closing_layernorm_gain).astype(jnp.bfloat16)
    normed_group = lax.all_gather(normed, "param", axis=0, tiled=True)
    head_cols = lax.all_gather(projection_weights_table, "batch", axis=0, tiled=True)
    raw_part = jnp.dot(normed_group, head_cols, preferred_element_type=jnp.float32)
    raw = lax.all_to_all(
        raw_part.astype(jnp.bfloat16), "param", split_axis=0, concat_axis=1, tiled=True
    )
    raw_f = raw.astype(jnp.float32)
    goal_scale = lax.rsqrt(jnp.sum(raw_f * raw_f, axis=1, keepdims=True) + 1e-06)
    goal_unit_f = raw_f * goal_scale
    target_normalized_vectors = goal_unit_f.astype(jnp.bfloat16)
    state_f = source_raw_vectors.astype(jnp.float32)
    state_inverse_norm = lax.rsqrt(jnp.sum(state_f * state_f, axis=1, keepdims=True) + 1e-06)
    state_unit_f = state_f * state_inverse_norm
    state_unit_embedding = state_unit_f.astype(jnp.bfloat16)
    target_vectors_gathered = lax.all_gather(target_normalized_vectors, "batch", axis=0, tiled=True)
    source_vectors_local, pos_group = (
        lax.all_gather(state_unit_embedding, "param", axis=0, tiled=True),
        lax.all_gather(matching_target_ids, "param", axis=0, tiled=True),
    )
    column = lax.iota(jnp.int32, batch_count * goal_rows)
    column_ids = (
        column // goal_rows * param_count + lax.axis_index("param")
    ) * goal_rows + column % goal_rows
    sharpness_multiplier = sharpness_parameter[0]
    shift_amount_value = similarity_shift_term[0]
    pair_similarity_scores = (
        sharpness_multiplier
        * jnp.dot(
            source_vectors_local, target_vectors_gathered.T, preferred_element_type=jnp.float32
        )
        + shift_amount_value
    )
    label_polarity = jnp.where(pos_group[:, None] == column_ids[None, :], 1.0, -1.0).astype(
        jnp.float32
    )
    coupling_coefficients = (
        -sharpness_multiplier
        * label_polarity
        * jax.nn.sigmoid(-label_polarity * pair_similarity_scores)
    ).astype(jnp.bfloat16)
    partial_states = jnp.dot(
        coupling_coefficients, target_vectors_gathered, preferred_element_type=jnp.float32
    )
    unit_state_grad = lax.psum_scatter(
        partial_states.astype(jnp.bfloat16), "param", scatter_dimension=0, tiled=True
    ).astype(jnp.float32)
    picked = coupling_coefficients
    unit_goal_grad = lax.psum_scatter(
        jnp.dot(picked.T, source_vectors_local, preferred_element_type=jnp.float32),
        "batch",
        scatter_dimension=0,
        tiled=True,
    )
    inner_s = jnp.sum(state_unit_f * unit_state_grad, axis=1, keepdims=True)
    state_grad = (state_inverse_norm * (unit_state_grad - state_unit_f * inner_s)).astype(
        jnp.bfloat16
    )
    inner_g = jnp.sum(goal_unit_f * unit_goal_grad, axis=1, keepdims=True)
    raw_grad = (goal_scale * (unit_goal_grad - goal_unit_f * inner_g)).astype(jnp.bfloat16)
    grad_cols = lax.all_to_all(raw_grad, "param", split_axis=1, concat_axis=0, tiled=True)
    picked = normed_group
    head_grad = lax.psum_scatter(
        jnp.dot(picked.T, grad_cols, preferred_element_type=jnp.float32),
        "batch",
        scatter_dimension=0,
        tiled=True,
    )
    return (state_grad, head_grad)


def solution(mesh):
    in_specs = (
        P(("batch", "param"), None),
        P(),
        P("batch", "param"),
        P(("batch", "param"), None),
        P(("batch", "param")),
        P(),
        P(),
    )
    out_specs = (P(("batch", "param"), None), P("batch", "param"))
    return jax.shard_map(body, mesh=mesh, in_specs=in_specs, out_specs=out_specs, check_vma=False)
```

profile of v0, /device:TPU:128, one launch (start us, length us, event | category | flops | bytes accessed | tf_op | source)
XLA Modules:
  0.0 1179.0 jit_solution(8311496987876735764)
XLA Ops:
  7.2 0.0 all-gather.3.cloned.1.call-start
  7.2 1.0 fusion.11
  8.3 1.7 fusion.10
  9.9 0.0 all-gather.3.cloned.1.call-update
  9.9 0.0 all-gather.5.cloned.1.call-start
  10.0 0.9 fusion.15
  10.9 0.8 fusion.17
  11.7 18.3 %all_gather.17 = bf16[64,2048]{1,0:T(8,128)(2,1)S(1)} all-gather(bf16[8,2048]{1,0:T(8,128)(2,1)S(1)} %fusion.17), channel_id=1, replica_groups=mesh['batch'=64,'param'=8] {'param'}, dimensions={0}, use_global_device_ids=true | all-gather | bytes 294912 | tf_op jit(solution)/shard_map/all_gather | solution.py:22
  30.0 159.7 %all_gather.18 = bf16[2048,128]{1,0:T(8,128)(2,1)S(1)} all-gather(bf16[32,128]{1,0:T(8,128)(2,1)} %param.9), channel_id=1, replica_groups=mesh['batch'=64,'param'=8] {'batch'}, dimensions={0}, use_global_device_ids=true | all-gather | bytes 532480 | tf_op jit(solution)/shard_map/all_gather | solution.py:23
  189.7 0.2 fusion.8
  190.0 10.7 all_to_all.32
  200.7 0.1 fusion.26
  200.8 0.7 fusion.21
  201.5 0.0 reduce-scatter.6.cloned.1.call-start
  202.8 1.3 dynamic-slice
  204.8 0.2 dynamic-update-slice
  205.0 9.2 all-reduce
  214.2 277.8 %all-gather.5.cloned.1.call-done = bf16[512,1024]{1,0:T(8,128)(2,1)} async-done(((bf16[8,1024]{1,0:T(8,128)(2,1)}), bf16[512,1024]{1,0:T(8,128)(2,1)}) %all-gather.5.cloned.1.call-update) | async-done | bytes 1048592 | tf_op jit(solution)/shard_map/all_gather | solution.py:36
  492.0 2.6 fusion.7
  494.7 2.1 fusion.41
  496.8 0.0 reduce-scatter.4.cloned.1.call-start
  496.8 1.7 convolution_convert_fusion
  498.6 0.0 reduce-scatter.8.cloned.1.call-start
  498.6 316.1 %reduce-scatter.6.cloned.1.call-done = f32[8,1024]{1,0:T(8,128)} async-done(((f32[512,1024]{1,0:T(8,128)}), f32[8,1024]{1,0:T(8,128)}) %reduce-scatter.6.cloned.1.call-update) | async-done | bytes 32784 | tf_op jit(solution)/shard_map/reduce_scatter | solution.py:69
  814.7 0.9 fusion.22
  815.6 0.8 fusion.27
  816.4 11.2 all_to_all.33
  827.6 1.3 fusion.28
  829.0 20.1 %reduce-scatter.4.cloned.1.call-done = bf16[64,1024]{1,0:T(8,128)(2,1)} async-done(((bf16[512,1024]{1,0:T(8,128)(2,1)}), bf16[64,1024]{1,0:T(8,128)(2,1)}) %reduce-scatter.4.cloned.1.call-update) | async-done | bytes 131088 | tf_op jit(solution)/shard_map/reduce_scatter | solution.py:65
  849.1 1.1 fusion.12
  850.2 1.7 fusion.14
  851.9 320.5 %reduce-scatter.8.cloned.1.call-done = f32[32,128]{1,0:T(8,128)} async-done(((f32[2048,128]{1,0:T(8,128)}), f32[32,128]{1,0:T(8,128)}) %reduce-scatter.8.cloned.1.call-update) | async-done | bytes 16400 | tf_op jit(solution)/shard_map/reduce_scatter | solution.py:83
  (18 shorter events, 0.1 us)
Async XLA Ops:
  7.2 197.6 %copy-start.3 = (s32[64]{0:T(128)S(1)}, s32[64]{0:T(128)}, u32[]{:S(2)}) copy-start(s32[64]{0:T(128)} %param.11) | copy-start | bytes 772
  7.2 207.1 %all-gather.3.cloned.1.call-start = ((), (), s32[]{:S(2)}) async-start(), calls=%async_computation.5 | async-start | bytes 1179648 | tf_op jit(solution)/shard_map/all_gather | solution.py:38
  9.9 482.0 %all-gather.5.cloned.1.call-start = ((), (), s32[]{:S(2)}) async-start(), calls=%async_computation.6 | async-start | bytes 1064960 | tf_op jit(solution)/shard_map/all_gather | solution.py:36
  201.5 613.2 %reduce-scatter.6.cloned.1.call-start = ((), (), s32[]{:S(2)}) async-start(), calls=%async_computation.8 | async-start | bytes 2129920 | tf_op jit(solution)/shard_map/reduce_scatter | solution.py:69
  492.0 2.7 copy-start.1
  494.7 2.2 copy-start.2
  496.8 352.3 %reduce-scatter.4.cloned.1.call-start = ((), (), s32[]{:S(2)}) async-start(), calls=%async_computation.7 | async-start | bytes 1179648 | tf_op jit(solution)/shard_map/reduce_scatter | solution.py:65
  498.5 350.6 %copy-start = (bf16[64,1024]{1,0:T(8,128)(2,1)S(1)}, bf16[64,1024]{1,0:T(8,128)(2,1)}, u32[]{:S(2)}) copy-start(bf16[64,1024]{1,0:T(8,128)(2,1)} %param.10) | copy-start | bytes 393220
  498.6 673.9 %reduce-scatter.8.cloned.1.call-start = ((), (), s32[]{:S(2)}) async-start(), calls=%async_computation.9 | async-start | bytes 1064960 | tf_op jit(solution)/shard_map/reduce_scatter | solution.py:83
Sparse Core Ops, SparseCore 0:
  10.7 35.5 all-gather.2
  201.6 290.3 all-gather.4
  496.9 317.7 reduce-scatter.5
  817.6 31.4 reduce-scatter.3
  852.5 319.8 reduce-scatter.7
where the time goes:
time: 1180 us
  waiting for transfers between devices  935 us (79%)
  blocking collectives  209 us (18%)
  between operations  15.8 us (1%)
    reduce_scatter x1, waiting for transfers between devices, body(): lax.psum_scatter(jnp.dot(picked.T, grad_cols, preferred_element_type=jnp....  321 us
    reduce_scatter x1, waiting for transfers between devices, body(): lax.psum_scatter(jnp.dot(picked.T, source_vectors_local, preferred_elemen...  316 us
    all_gather x1, waiting for transfers between devices, body(): lax.all_gather(target_normalized_vectors, 'batch', axis=0, tiled=True)  278 us
    all_gather x1, blocking collectives, body(): lax.all_gather(projection_weights_table, 'batch', axis=0, tiled=True)  160 us
  transfers between devices with their start and end apart: 5, of which 4 were waited for; matrix products, arithmetic and copies ran while one was open for 1% of the time, Pallas kernels for 0%

commit v1 on v0

v1 whole, which is shorter than its diff:
```python
import jax
import jax.numpy as jnp
from jax import lax
from jax.experimental import pallas as pl
from jax.experimental.pallas import tpu as pltpu
from jax.sharding import PartitionSpec as P

F32 = jnp.float32
BF16 = jnp.bfloat16
MESH = pl.DeviceIdType.MESH
NX, NY, NZ = 4, 8, 8
N_SEM = 160
FAR_Y = (4, 3, 5, 2, 6, 1, 7)
FAR_X = (2, 1, 3)


def dot(a, b, contract=((1,), (0,))):
    return lax.dot_general(a, b, (contract, ((), ())), preferred_element_type=F32)


def kernel(
    feat, gain, wblk, src, idrow, sharp, shift,
    sg_out, hg_out,
    nbuf, wbuf, rpart, rbuf, gown, gbuf, sbuf, idbuf, pt,
    uown, usend, urecv, ub, ua1, ub1, ta, tb, ua2, ub2, xbuf,
    rgb, rgr, hbuf, ha1, hb1, hta, htb, ha2, hb2, hz, hzr,
    spbuf, srecv, send_sem, recv_sem,
):
    b = lax.axis_index("batch")
    p = lax.axis_index("param")
    zlo = b // 32
    x = lax.rem(b // 8, NX)
    y = lax.rem(b, NY)
    zhi = p // 2
    core = lax.rem(p, 2)
    z = zhi * 2 + zlo

    def dev(x=x, y=y, z=z, core=core):
        return (lax.rem(z, 2) * 32 + x * 8 + y, (z // 2) * 2 + core)

    def xd(d):
        return lax.rem(x + d, NX)

    def yd(d):
        return lax.rem(y + d, NY)

    def zd(d):
        return lax.rem(z + d, NZ)

    peers = [dev(y=yd(d)) for d in range(1, NY)]
    peers += [dev(x=xd(d)) for d in range(1, NX)]
    peers += [dev(z=zd(d)) for d in range(1, NZ)]
    peers += [dev(z=zd(d), core=1 - core) for d in (0, 2, 4, 6)]
    barrier = pltpu.get_barrier_semaphore()
    for peer in peers:
        pl.semaphore_signal(barrier, inc=1, device_id=peer, device_id_type=MESH)

    f = feat[...].astype(F32)
    nf = f * lax.rsqrt(jnp.mean(f * f, axis=1, keepdims=True) + 1e-6) * gain[...]
    nbuf[zhi, core] = jnp.concatenate([nf[:, :1024], nf[:, 1024:]], axis=0).astype(BF16)
    wbuf[x, y, pl.ds(pl.multiple_of(zlo * 32, 32), 32), :] = wblk[...]
    idbuf[z] = idrow[...]
    s_f = src[...].astype(F32)
    s_scale = lax.rsqrt(jnp.sum(s_f * s_f, axis=1, keepdims=True) + 1e-6)
    s_unit = (s_f * s_scale).astype(BF16)
    sbuf[0, z] = s_unit[:, :512]
    sbuf[1, z] = s_unit[:, 512:]

    pl.semaphore_wait(barrier, len(peers))

    started = []

    def cp(a, c, device):
        i = len(started)
        copy = pltpu.make_async_remote_copy(
            src_ref=a, dst_ref=c, send_sem=send_sem.at[i], recv_sem=recv_sem.at[i],
            device_id=device, device_id_type=MESH,
        )
        copy.start()
        started.append(copy)
        return copy

    def arrived(copies):
        for copy in copies:
            copy.wait_recv()

    def over_x(src_of, dst_of):
        return [cp(src_of(xd(d)), dst_of(d), dev(x=xd(d))) for d in FAR_X]

    def over_y(src_of, dst_of):
        return [cp(src_of(yd(d)), dst_of(d), dev(y=yd(d))) for d in FAR_Y]

    wz = wbuf.at[x, y, pl.ds(pl.multiple_of(zlo * 32, 32), 32), :]
    c_wz = cp(wz, wz, dev(z=z + 1 - 2 * zlo))
    c_n = [cp(nbuf.at[zhi, core], nbuf.at[zhi, core], dev(z=zd(d))) for d in (4, 2, 6)]
    c_wz.wait_recv()
    wa, wb = pl.ds(0, 16), pl.ds(16, 48)
    w1a = over_x(lambda t: wbuf.at[x, y, wa], lambda d: wbuf.at[x, y, wa])
    w1b = over_y(lambda t: wbuf.at[x, y, wb], lambda d: wbuf.at[x, y, wb])

    def hop(block, rows, step):
        ref = sbuf.at[:, block, rows]
        return cp(ref, ref, dev(z=zd(step)))

    every, low, high = pl.ds(0, 64), pl.ds(0, 32), pl.ds(32, 32)
    s_up, s_down = hop(z, every, 1), hop(z, every, 7)
    c_id = [cp(idbuf.at[z], idbuf.at[z], dev(z=zd(d))) for d in range(1, NZ)]

    arrived(w1a)
    w2a = over_y(lambda t: wbuf.at[:, y, wa], lambda d: wbuf.at[:, y, wa])
    arrived(w1b)
    w2b = over_x(lambda t: wbuf.at[x, :, wb], lambda d: wbuf.at[x, :, wb])
    arrived(c_n)
    c_ns = cp(nbuf.at[:, core], nbuf.at[:, core], dev(core=1 - core))
    s_up.wait_recv()
    s_down.wait_recv()
    s_up, s_down = hop(zd(7), every, 1), hop(zd(1), every, 7)
    c_ns.wait_recv()
    arrived(w2a)
    arrived(w2b)

    normed = nbuf[...].reshape(128, 1024)
    top = dot(normed, wbuf[:, :, 0:32, :].reshape(1024, 128)).reshape(8, 16, 128)
    bottom = dot(normed, wbuf[:, :, 32:64, :].reshape(1024, 128)).reshape(8, 16, 128)
    rpart[...] = (top[:, 0:8] + bottom[:, 8:16]).reshape(4, 16, 128).astype(BF16)
    rbuf[p] = rpart[zhi]
    c_r = []
    for d in (4, 2, 6, 0):
        to = zd(d)
        if d:
            c_r.append(cp(rpart.at[to // 2], rbuf.at[p], dev(z=to)))
        c_r.append(cp(rpart.at[to // 2], rbuf.at[p], dev(z=to, core=1 - core)))
    arrived(c_r)

    raw_f = jnp.concatenate([rbuf[k] for k in range(8)], axis=1).astype(F32)
    g_scale = lax.rsqrt(jnp.sum(raw_f * raw_f, axis=1, keepdims=True) + 1e-6)
    g_unit = (raw_f * g_scale).astype(BF16)
    gown[0] = g_unit[:, :512]
    gown[1] = g_unit[:, 512:]
    gbuf[core, x, y] = gown[core]
    ga, gb = pl.ds(0, 128), pl.ds(128, 384)
    g1a = over_x(lambda t: gbuf.at[core, x, y, :, ga], lambda d: gbuf.at[core, x, y, :, ga])
    g1b = over_y(lambda t: gbuf.at[core, x, y, :, gb], lambda d: gbuf.at[core, x, y, :, gb])
    s_up.wait_recv()
    s_down.wait_recv()
    s_up, s_down = hop(zd(6), every, 1), hop(zd(2), every, 7)
    arrived(g1a)
    g2a = over_y(lambda t: gbuf.at[core, :, y, :, ga], lambda d: gbuf.at[core, :, y, :, ga])
    arrived(g1b)
    g2b = over_x(lambda t: gbuf.at[core, x, :, :, gb], lambda d: gbuf.at[core, x, :, :, gb])
    s_up.wait_recv()
    s_down.wait_recv()
    s_up, s_down = hop(zd(5), low, 1), hop(zd(3), high, 7)
    arrived(g2a)
    arrived(g2b)
    c_g = cp(gbuf.at[core], gbuf.at[core], dev(core=1 - core))
    arrived(c_id)
    s_up.wait_recv()
    s_down.wait_recv()
    c_g.wait_recv()

    scale, offset = sharp[0], shift[0]
    ids = jnp.concatenate(
        [idbuf[2 * q, 0:1] + idbuf[2 * q + 1, 0:1] for q in range(4)], axis=1
    )
    row = lax.broadcasted_iota(jnp.int32, (128, 1), 0)

    def goals_step(k, carry):
        s0 = sbuf[0].reshape(512, 512)
        s1 = sbuf[1].reshape(512, 512)
        nt = ((1,), (1,))
        sim = dot(gbuf[0, k].reshape(128, 512), s0, nt) + dot(gbuf[1, k].reshape(128, 512), s1, nt)
        logits = scale * sim + offset
        goal = (lax.rem(z, 2) * 32 + k * 8 + row // 16) * 64 + zhi * 16 + lax.rem(row, 16)
        sign = jnp.where(goal == ids, 1.0, -1.0).astype(F32)
        weight = (-scale * sign / (1.0 + jnp.exp(sign * logits))).astype(BF16)
        pt[pl.ds(pl.multiple_of(k * 128, 128), 128), :] = weight
        uown[k] = dot(weight, sbuf[core].reshape(512, 512)).reshape(8, 16, 512)
        usend[k] = dot(weight, sbuf[1 - core].reshape(512, 512)).reshape(8, 16, 512).astype(BF16)
        return carry

    lax.fori_loop(0, NX, goals_step, 0)
    c_u = cp(usend, urecv, dev(core=1 - core))

    for q in range(4):
        lhs = pt[:, q * 128:(q + 1) * 128]
        for h in range(2):
            part = dot(lhs, gbuf[h].reshape(512, 512), ((0,), (0,)))
            spbuf[2 * q:2 * q + 2, h] = part.reshape(2, 64, 512).astype(BF16)

    c_u.wait_recv()
    for k in range(NX):
        ub[k] = (uown[k] + urecv[k].astype(F32)).astype(BF16)
    u1a = over_y(lambda t: ub.at[:, t, :, ga], lambda d: ua1.at[d - 1])
    u1b = over_x(lambda t: ub.at[t, :, :, gb], lambda d: ub1.at[d - 1])
    c_s = [cp(spbuf.at[zd(d)], srecv.at[d - 1], dev(z=zd(d))) for d in (4, 3, 5, 2, 6, 1, 7)]
    arrived(u1a)
    ta[...] = (ub[:, y, :, 0:128].astype(F32) + jnp.sum(ua1[...].astype(F32), axis=0)).astype(BF16)
    u2a = over_x(lambda t: ta.at[t], lambda d: ua2.at[d - 1])
    arrived(u1b)
    tb[...] = (ub[x, :, :, 128:512].astype(F32) + jnp.sum(ub1[...].astype(F32), axis=0)).astype(BF16)
    u2b = over_y(lambda t: tb.at[t], lambda d: ub2.at[d - 1])
    arrived(u2a)
    xbuf[core, :, 0:128] = ta[x].astype(F32) + jnp.sum(ua2[...].astype(F32), axis=0)
    arrived(u2b)
    xbuf[core, :, 128:512] = tb[y].astype(F32) + jnp.sum(ub2[...].astype(F32), axis=0)
    c_x = cp(xbuf.at[core], xbuf.at[core], dev(core=1 - core))
    c_x.wait_recv()

    u = jnp.concatenate([xbuf[0], xbuf[1]], axis=1)
    g_f = raw_f * g_scale
    inner = jnp.sum(g_f * u, axis=1, keepdims=True)
    raw_grad = (g_scale * (u - g_f * inner)).astype(BF16)
    for k in range(8):
        rgb[k] = raw_grad[:, k * 128:(k + 1) * 128]
    rgr[zhi] = rgb[p]
    c_rg = [cp(rgb.at[(zd(d) // 2) * 2 + core], rgr.at[zhi], dev(z=zd(d))) for d in (4, 2, 6)]
    arrived(c_rg)
    rg = rgr[...].astype(F32).reshape(8, 8, 128)
    zero = jnp.zeros((8, 8, 128), F32)
    rg_top = jnp.concatenate([rg, zero], axis=1).reshape(128, 128).astype(BF16)
    rg_bottom = jnp.concatenate([zero, rg], axis=1).reshape(128, 128).astype(BF16)
    normed = nbuf[...].reshape(128, 1024)
    tn = ((0,), (0,))
    hbuf[:, :, 0:32, :] = dot(normed, rg_top, tn).reshape(4, 8, 32, 128).astype(BF16)
    hbuf[:, :, 32:64, :] = dot(normed, rg_bottom, tn).reshape(4, 8, 32, 128).astype(BF16)
    h1a = over_y(lambda t: hbuf.at[:, t, wa], lambda d: ha1.at[d - 1])
    h1b = over_x(lambda t: hbuf.at[t, :, wb], lambda d: hb1.at[d - 1])
    arrived(h1a)
    hta[...] = (hbuf[:, y, 0:16].astype(F32) + jnp.sum(ha1[...].astype(F32), axis=0)).astype(BF16)
    h2a = over_x(lambda t: hta.at[t], lambda d: ha2.at[d - 1])
    arrived(h1b)
    htb[...] = (hbuf[x, :, 16:64].astype(F32) + jnp.sum(hb1[...].astype(F32), axis=0)).astype(BF16)
    h2b = over_y(lambda t: htb.at[t], lambda d: hb2.at[d - 1])
    arrived(h2a)
    h_a = hta[x].astype(F32) + jnp.sum(ha2[...].astype(F32), axis=0)
    arrived(h2b)
    h_b = htb[y].astype(F32) + jnp.sum(hb2[...].astype(F32), axis=0)
    hz[0, 0:16] = h_a
    hz[0, 16:32] = h_b[0:16]
    hz[1] = h_b[16:48]
    c_h = cp(hz.at[1 - zlo], hzr, dev(z=z + 1 - 2 * zlo))

    arrived(c_s)
    su_f = s_f * s_scale
    g0 = spbuf[z, 0].astype(F32)
    g1 = spbuf[z, 1].astype(F32)
    for d in range(7):
        g0 += srecv[d, 0].astype(F32)
        g1 += srecv[d, 1].astype(F32)
    usg = jnp.concatenate([g0, g1], axis=1)
    inner_s = jnp.sum(su_f * usg, axis=1, keepdims=True)
    sg_out[...] = (s_scale * (usg - su_f * inner_s)).astype(BF16)

    c_h.wait_recv()
    hg_out[...] = hz[zlo] + hzr[...]
    for copy in started:
        copy.wait_send()


def body(features, gain, weights, states, ids, sharpness, offset):
    core = lax.rem(lax.axis_index("param"), 2)
    z = (lax.axis_index("param") // 2) * 2 + lax.axis_index("batch") // 32
    lane = lax.broadcasted_iota(jnp.int32, (8, 128), 1)
    twice = jnp.concatenate([ids, ids])[None, :]
    idrow = jnp.where(lane // 64 == lax.rem(z, 2), twice, 0)
    vmem = pl.BlockSpec(memory_space=pltpu.VMEM)
    smem = pl.BlockSpec(memory_space=pltpu.SMEM)
    V = pltpu.VMEM
    return pl.pallas_call(
        kernel,
        out_shape=(
            jax.ShapeDtypeStruct((64, 1024), BF16),
            jax.ShapeDtypeStruct((32, 128), F32),
        ),
        in_specs=[vmem] * 5 + [smem] * 2,
        out_specs=(vmem, vmem),
        scratch_shapes=[
            V((4, 2, 16, 1024), BF16),
            V((4, 8, 64, 128), BF16),
            V((4, 16, 128), BF16),
            V((8, 16, 128), BF16),
            V((2, 16, 512), BF16),
            V((2, 4, 8, 16, 512), BF16),
            V((2, 8, 64, 512), BF16),
            V((8, 8, 128), jnp.int32),
            V((512, 512), BF16),
            V((4, 8, 16, 512), F32),
            V((4, 8, 16, 512), BF16),
            V((4, 8, 16, 512), BF16),
            V((4, 8, 16, 512), BF16),
            V((7, 4, 16, 128), BF16),
            V((3, 8, 16, 384), BF16),
            V((4, 16, 128), BF16),
            V((8, 16, 384), BF16),
            V((3, 16, 128), BF16),
            V((7, 16, 384), BF16),
            V((2, 16, 512), F32),
            V((8, 16, 128), BF16),
            V((4, 16, 128), BF16),
            V((4, 8, 64, 128), BF16),
            V((7, 4, 16, 128), BF16),
            V((3, 8, 48, 128), BF16),
            V((4, 16, 128), BF16),
            V((8, 48, 128), BF16),
            V((3, 16, 128), BF16),
            V((7, 48, 128), BF16),
            V((2, 32, 128), F32),
            V((32, 128), F32),
            V((8, 2, 64, 512), BF16),
            V((7, 2, 64, 512), BF16),
            pltpu.SemaphoreType.DMA((N_SEM,)),
            pltpu.SemaphoreType.DMA((N_SEM,)),
        ],
        compiler_params=pltpu.CompilerParams(
            collective_id=0, has_side_effects=True, vmem_limit_bytes=48 * 2**20
        ),
    )(features, gain.reshape(1, 2048), weights, states, idrow, sharpness, offset)


def solution(mesh):
    in_specs = (
        P(("batch", "param"), None),
        P(),
        P("batch", "param"),
        P(("batch", "param"), None),
        P(("batch", "param")),
        P(),
        P(),
    )
    out_specs = (P(("batch", "param"), None), P("batch", "param"))
    return jax.shard_map(body, mesh=mesh, in_specs=in_specs, out_specs=out_specs, check_vma=False)
```

time: 1180 us -> 96.8 us (0.08)
  the two profiles are of different devices: /device:TPU:128 before, /device:TPU:1 now
where the time goes in v1:
time: 96.8 us; the launch traced here: 96.5 us
  Pallas kernels  91.6 us (95%)
  local copies, waits for them, and re-layouts  2.75 us (3%)
  between operations  2.03 us (2%)
    pallas_call x1, Pallas kernels, body(): pl.pallas_call(kernel, out_shape=(jax.ShapeDtypeStruct((64, 1024), BF16),...  91.6 us
    unnamed x12, local copies, waits for them, and re-layouts  2.75 us

profile of v1, /device:TPU:1, one launch (start us, length us, event | category | flops | bytes accessed | tf_op | source)
XLA Modules:
  0.0 96.5 jit_solution(9583880312916958946)
XLA Ops:
  0.6 0.0 copy-start.1
  1.3 0.0 copy-start.4
  2.0 0.0 copy-start.3
  2.0 0.0 copy-start.2
  2.0 0.0 copy-done.4
  2.0 0.1 iota_shift-right-logical_fusion
  2.1 0.0 copy-done.1
  2.1 0.6 copy-done.3
  2.7 0.0 copy-done.2
  2.7 0.0 copy-start
  2.7 0.9 copy-done
  3.6 91.6 %shard_map.86 = (bf16[64,1024]{1,0:T(8,128)(2,1)S(1)}, f32[32,128]{1,0:T(8,128)S(1)}) custom-call(bf16[8,2048]{1,0:T(8,128)(2,1)S(1)} %copy-done.1, f32[1,2048]{1,0:T(1,128)S(1)} %bitcast.1, bf16[32,128]{1,0:T(8,128)(2,1)S(1)} %copy-done.3, bf16[64,1024]{1,0:T(8,128)(2,1)S(1)} %copy-done, s32[8,128]{1,0:T(8,128)S(1)} %fusion.idrow, f32[1]{0:T(128)S(6)} %copy.11.sharp, ...), custom_call_target="tpu_custom_call" | custom-call | tf_op jit(solution)/shard_map/pallas_call | solution.py:270
  95.2 0.7 copy.13
  95.9 0.6 copy.14
  (3 shorter events, 0.0 us)
Async XLA Ops:
  0.6 1.5 %copy-start.1 = (bf16[8,2048]{1,0:T(8,128)(2,1)S(1)}, bf16[8,2048]{1,0:T(8,128)(2,1)}, u32[]{:S(2)}) copy-start(bf16[8,2048]{1,0:T(8,128)(2,1)} %feat.1) | copy-start | bytes 98308
  1.3 0.7 copy-start.4
  2.0 0.7 copy-start.3
  2.0 0.7 copy-start.2
  2.7 0.9 copy-start

commit v2 on v1

--- a/solution.py
+++ b/solution.py
@@ -19,12 +19,12 @@
 
 
 def kernel(
-    feat, gain, wblk, src, idrow, sharp, shift,
+    feat_in, gain_in, wblk_in, src_in, idrow_in, sharp, shift,
     sg_out, hg_out,
-    nbuf, wbuf, rpart, rbuf, gown, gbuf, sbuf, idbuf, pt,
+    feat, gain, wblk, src, idrow, nbuf, wbuf, rpart, rbuf, gown, gbuf, sbuf, idbuf, pt,
     uown, usend, urecv, ub, ua1, ub1, ta, tb, ua2, ub2, xbuf,
     rgb, rgr, hbuf, ha1, hb1, hta, htb, ha2, hb2, hz, hzr,
-    spbuf, srecv, send_sem, recv_sem,
+    spbuf, srecv, send_sem, recv_sem, in_sem,
 ):
     b = lax.axis_index("batch")
     p = lax.axis_index("param")
@@ -47,6 +47,15 @@
     def zd(d):
         return lax.rem(z + d, NZ)
 
+    loads = [
+        pltpu.make_async_copy(a, c, in_sem.at[i])
+        for i, (a, c) in enumerate(
+            ((wblk_in, wblk), (feat_in, feat), (gain_in, gain), (src_in, src), (idrow_in, idrow))
+        )
+    ]
+    for load in loads:
+        load.start()
+
     peers = [dev(y=yd(d)) for d in range(1, NY)]
     peers += [dev(x=xd(d)) for d in range(1, NX)]
     peers += [dev(z=zd(d)) for d in range(1, NZ)]
@@ -55,6 +64,8 @@
     for peer in peers:
         pl.semaphore_signal(barrier, inc=1, device_id=peer, device_id_type=MESH)
 
+    for load in loads:
+        load.wait()
     f = feat[...].astype(F32)
     nf = f * lax.rsqrt(jnp.mean(f * f, axis=1, keepdims=True) + 1e-6) * gain[...]
     nbuf[zhi, core] = jnp.concatenate([nf[:, :1024], nf[:, 1024:]], axis=0).astype(BF16)
@@ -147,40 +158,65 @@
     arrived(g1a)
     g2a = over_y(lambda t: gbuf.at[core, :, y, :, ga], lambda d: gbuf.at[core, :, y, :, ga])
     arrived(g1b)
-    g2b = over_x(lambda t: gbuf.at[core, x, :, :, gb], lambda d: gbuf.at[core, x, :, :, gb])
+    mine = gbuf.at[core, x, :, :, gb]
+    g2b = {d: cp(mine, mine, dev(x=xd(d))) for d in FAR_X}
     s_up.wait_recv()
     s_down.wait_recv()
     s_up, s_down = hop(zd(5), low, 1), hop(zd(3), high, 7)
     arrived(g2a)
-    arrived(g2b)
-    c_g = cp(gbuf.at[core], gbuf.at[core], dev(core=1 - core))
+
+    sibling = dev(core=1 - core)
+    c_g, c_u, u1b = {}, {}, []
+
+    def share(d):
+        if d:
+            g2b[NX - d].wait_recv()
+        block = gbuf.at[core, xd(d)]
+        c_g[d] = cp(block, block, sibling)
+
+    def weigh(d):
+        k = xd(d)
+        c_g[d].wait_recv()
+        nt = ((1,), (1,))
+        sim = dot(gbuf[0, k].reshape(128, 512), sbuf[0].reshape(512, 512), nt)
+        sim += dot(gbuf[1, k].reshape(128, 512), sbuf[1].reshape(512, 512), nt)
+        logits = scale * sim + offset
+        goal = (zlo * 32 + k * 8 + row // 16) * 64 + zhi * 16 + lax.rem(row, 16)
+        sign = jnp.where(goal == ids, 1.0, -1.0).astype(F32)
+        weight = (-scale * sign / (1.0 + jnp.exp(sign * logits))).astype(BF16)
+        pt[pl.ds(pl.multiple_of(k * 128, 128), 128), :] = weight
+        usend[k] = dot(weight, sbuf[1 - core].reshape(512, 512)).reshape(8, 16, 512).astype(BF16)
+        c_u[d] = cp(usend.at[k], urecv.at[k], sibling)
+        uown[k] = dot(weight, sbuf[core].reshape(512, 512)).reshape(8, 16, 512)
+
+    def pass_on(d):
+        k = xd(d)
+        c_u[d].wait_recv()
+        ub[k] = (uown[k] + urecv[k].astype(F32)).astype(BF16)
+        if d:
+            u1b.append(cp(ub.at[k, :, :, gb], ub1.at[d - 1], dev(x=k)))
+
+    share(0)
+    scale, offset = sharp[0], shift[0]
+    row = lax.broadcasted_iota(jnp.int32, (128, 1), 0)
     arrived(c_id)
-    s_up.wait_recv()
-    s_down.wait_recv()
-    c_g.wait_recv()
-
-    scale, offset = sharp[0], shift[0]
     ids = jnp.concatenate(
         [idbuf[2 * q, 0:1] + idbuf[2 * q + 1, 0:1] for q in range(4)], axis=1
     )
-    row = lax.broadcasted_iota(jnp.int32, (128, 1), 0)
-
-    def goals_step(k, carry):
-        s0 = sbuf[0].reshape(512, 512)
-        s1 = sbuf[1].reshape(512, 512)
-        nt = ((1,), (1,))
-        sim = dot(gbuf[0, k].reshape(128, 512), s0, nt) + dot(gbuf[1, k].reshape(128, 512), s1, nt)
-        logits = scale * sim + offset
-        goal = (lax.rem(z, 2) * 32 + k * 8 + row // 16) * 64 + zhi * 16 + lax.rem(row, 16)
-        sign = jnp.where(goal == ids, 1.0, -1.0).astype(F32)
-        weight = (-scale * sign / (1.0 + jnp.exp(sign * logits))).astype(BF16)
-        pt[pl.ds(pl.multiple_of(k * 128, 128), 128), :] = weight
-        uown[k] = dot(weight, sbuf[core].reshape(512, 512)).reshape(8, 16, 512)
-        usend[k] = dot(weight, sbuf[1 - core].reshape(512, 512)).reshape(8, 16, 512).astype(BF16)
-        return carry
-
-    lax.fori_loop(0, NX, goals_step, 0)
-    c_u = cp(usend, urecv, dev(core=1 - core))
+    s_up.wait_recv()
+    s_down.wait_recv()
+    share(1)
+    weigh(0)
+    share(3)
+    weigh(1)
+    pass_on(0)
+    share(2)
+    weigh(3)
+    pass_on(1)
+    weigh(2)
+    pass_on(3)
+    pass_on(2)
+    u1a = over_y(lambda t: ub.at[:, t, :, ga], lambda d: ua1.at[d - 1])
 
     for q in range(4):
         lhs = pt[:, q * 128:(q + 1) * 128]
@@ -188,12 +224,10 @@
             part = dot(lhs, gbuf[h].reshape(512, 512), ((0,), (0,)))
             spbuf[2 * q:2 * q + 2, h] = part.reshape(2, 64, 512).astype(BF16)
 
-    c_u.wait_recv()
-    for k in range(NX):
-        ub[k] = (uown[k] + urecv[k].astype(F32)).astype(BF16)
-    u1a = over_y(lambda t: ub.at[:, t, :, ga], lambda d: ua1.at[d - 1])
-    u1b = over_x(lambda t: ub.at[t, :, :, gb], lambda d: ub1.at[d - 1])
-    c_s = [cp(spbuf.at[zd(d)], srecv.at[d - 1], dev(z=zd(d))) for d in (4, 3, 5, 2, 6, 1, 7)]
+    def scatter_states(ds):
+        return [cp(spbuf.at[zd(d)], srecv.at[d - 1], dev(z=zd(d))) for d in ds]
+
+    c_s = scatter_states((3, 5, 1, 7))
     arrived(u1a)
     ta[...] = (ub[:, y, :, 0:128].astype(F32) + jnp.sum(ua1[...].astype(F32), axis=0)).astype(BF16)
     u2a = over_x(lambda t: ta.at[t], lambda d: ua2.at[d - 1])
@@ -215,6 +249,7 @@
         rgb[k] = raw_grad[:, k * 128:(k + 1) * 128]
     rgr[zhi] = rgb[p]
     c_rg = [cp(rgb.at[(zd(d) // 2) * 2 + core], rgr.at[zhi], dev(z=zd(d))) for d in (4, 2, 6)]
+    c_s += scatter_states((4, 2, 6))
     arrived(c_rg)
     rg = rgr[...].astype(F32).reshape(8, 8, 128)
     zero = jnp.zeros((8, 8, 128), F32)
@@ -265,6 +300,7 @@
     twice = jnp.concatenate([ids, ids])[None, :]
     idrow = jnp.where(lane // 64 == lax.rem(z, 2), twice, 0)
     vmem = pl.BlockSpec(memory_space=pltpu.VMEM)
+    hbm = pl.BlockSpec(memory_space=pltpu.HBM)
     smem = pl.BlockSpec(memory_space=pltpu.SMEM)
     V = pltpu.VMEM
     return pl.pallas_call(
@@ -273,9 +309,14 @@
             jax.ShapeDtypeStruct((64, 1024), BF16),
             jax.ShapeDtypeStruct((32, 128), F32),
         ),
-        in_specs=[vmem] * 5 + [smem] * 2,
+        in_specs=[hbm] * 5 + [smem] * 2,
         out_specs=(vmem, vmem),
         scratch_shapes=[
+            V((8, 2048), BF16),
+            V((1, 2048), F32),
+            V((32, 128), BF16),
+            V((64, 1024), BF16),
+            V((8, 128), jnp.int32),
             V((4, 2, 16, 1024), BF16),
             V((4, 8, 64, 128), BF16),
             V((4, 16, 128), BF16),
@@ -311,6 +352,7 @@
             V((7, 2, 64, 512), BF16),
             pltpu.SemaphoreType.DMA((N_SEM,)),
             pltpu.SemaphoreType.DMA((N_SEM,)),
+            pltpu.SemaphoreType.DMA((5,)),
         ],
         compiler_params=pltpu.CompilerParams(
             collective_id=0, has_side_effects=True, vmem_limit_bytes=48 * 2**20

time: 96.8 us -> 88.3 us (0.912)
  Pallas kernels: 91.6 us -> 82.3 us
    pallas_call x1, Pallas kernels: 91.6 us -> 82.3 us  [body(): pl.pallas_call(kernel, out_shape=(jax.ShapeDtypeStruct((64, 1024), BF16),...]
where the time goes in v2:
time: 88.3 us; the launch traced here: 87.2 us
  Pallas kernels  82.3 us (93%)
  local copies, waits for them, and re-layouts  2.75 us (3%)
  between operations  2.03 us (2%)
    pallas_call x1, Pallas kernels, body(): pl.pallas_call(kernel, out_shape=(jax.ShapeDtypeStruct((64, 1024), BF16),...  82.3 us
    unnamed x12, local copies, waits for them, and re-layouts  2.75 us

profile of v2, /device:TPU:1, one launch (start us, length us, event | category | flops | bytes accessed | tf_op | source)
XLA Modules:
  0.0 87.2 jit_solution(13633061125857032728)
XLA Ops:
  0.6 0.0 copy-start.1
  1.3 0.0 copy-start.4
  2.0 0.0 copy-start.3
  2.0 0.0 copy-start.2
  2.0 0.0 copy-done.4
  2.0 0.1 iota_shift-right-logical_fusion
  2.1 0.0 copy-done.1
  2.1 0.6 copy-done.3
  2.7 0.0 copy-done.2
  2.7 0.0 copy-start
  2.7 0.9 %copy-done = bf16[64,1024]{1,0:T(8,128)(2,1)S(1)} copy-done((bf16[64,1024]{1,0:T(8,128)(2,1)S(1)}, bf16[64,1024]{1,0:T(8,128)(2,1)}, u32[]{:S(2)}) %copy-start) | copy-done | bytes 131096
  3.6 82.3 %shard_map.86 = (bf16[64,1024]{1,0:T(8,128)(2,1)S(1)}, f32[32,128]{1,0:T(8,128)S(1)}) custom-call(bf16[8,2048]{1,0:T(8,128)(2,1)S(1)} %copy-done.1, f32[1,2048]{1,0:T(1,128)S(1)} %bitcast.1, bf16[32,128]{1,0:T(8,128)(2,1)S(1)} %copy-done.3, bf16[64,1024]{1,0:T(8,128)(2,1)S(1)} %copy-done, s32[8,128]{1,0:T(8,128)S(1)} %fusion.idrow_in, f32[1]{0:T(128)S(6)} %copy.11.sharp, ...), custom_call_target="tpu_custom_call" | custom-call | tf_op jit(solution)/shard_map/pallas_call | solution.py:306
  85.9 0.7 copy.13
  86.6 0.6 copy.14
  (3 shorter events, 0.0 us)
Async XLA Ops:
  0.6 1.5 %copy-start.1 = (bf16[8,2048]{1,0:T(8,128)(2,1)S(1)}, bf16[8,2048]{1,0:T(8,128)(2,1)}, u32[]{:S(2)}) copy-start(bf16[8,2048]{1,0:T(8,128)(2,1)} %feat_in.1) | copy-start | bytes 98308
  1.3 0.7 copy-start.4
  2.0 0.7 copy-start.3
  2.0 0.7 copy-start.2
  2.7 0.9 %copy-start = (bf16[64,1024]{1,0:T(8,128)(2,1)S(1)}, bf16[64,1024]{1,0:T(8,128)(2,1)}, u32[]{:S(2)}) copy-start(bf16[64,1024]{1,0:T(8,128)(2,1)} %src_in.1) | copy-start | bytes 393220

commit v3 on v2

v3 whole, which is shorter than its diff:
```python
import jax
import jax.numpy as jnp
from jax import lax
from jax.experimental import pallas as pl
from jax.experimental.pallas import tpu as pltpu
from jax.sharding import PartitionSpec as P

F32 = jnp.float32
BF16 = jnp.bfloat16
MESH = pl.DeviceIdType.MESH
NX, NY, NZ = 4, 8, 8
N_SEM = 208
FAR_Y = (4, 3, 5, 2, 6, 1, 7)
FAR_X = (2, 1, 3)


def dot(a, b, contract=((1,), (0,))):
    return lax.dot_general(a, b, (contract, ((), ())), preferred_element_type=F32)


def kernel(
    feat_in, gain_in, wblk_in, src_in, idrow_in, sharp, shift,
    sg_out, hg_out,
    feat, gain, wblk, src, idrow, nsend, nq, wq, rpart, rbuf, gown, gbuf, sbuf, idbuf, pt,
    uown, usend, urecv, ub, ua1, ub1, ta, tb, ua2, ub2, xbuf,
    rgb, rgr, nt_buf, hq, hsum,
    spbuf, shalf, srecv, send_sem, recv_sem, in_sem,
):
    b = lax.axis_index("batch")
    p = lax.axis_index("param")
    zlo = b // 32
    x = lax.rem(b // 8, NX)
    y = lax.rem(b, NY)
    zhi = p // 2
    core = lax.rem(p, 2)
    z = zhi * 2 + zlo
    zp = z + 1 - 2 * zlo

    def dev(x=x, y=y, z=z, core=core):
        return (lax.rem(z, 2) * 32 + x * 8 + y, (z // 2) * 2 + core)

    def xd(d):
        return lax.rem(x + d, NX)

    def yd(d):
        return lax.rem(y + d, NY)

    def zd(d):
        return lax.rem(z + d, NZ)

    loads = [
        pltpu.make_async_copy(a, c, in_sem.at[i])
        for i, (a, c) in enumerate(
            ((wblk_in, wblk), (feat_in, feat), (gain_in, gain), (src_in, src), (idrow_in, idrow))
        )
    ]
    for load in loads:
        load.start()

    peers = [dev(y=yd(d)) for d in range(1, NY)]
    peers += [dev(y=yd(d), z=zp) for d in range(1, NY)]
    peers += [dev(z=zd(d)) for d in range(1, NZ)]
    peers += [dev(x=xd(d), z=zd(e)) for d in (1, 2, 3) for e in (0, 2, 4, 6)]
    peers += [dev(x=xd(d), z=zd(e), core=1 - core) for d in (0, 1, 2, 3) for e in (0, 2, 4, 6)]
    barrier = pltpu.get_barrier_semaphore()
    for peer in peers:
        pl.semaphore_signal(barrier, inc=1, device_id=peer, device_id_type=MESH)

    for load in loads:
        load.wait()
    f = feat[...].astype(F32)
    nf = f * lax.rsqrt(jnp.mean(f * f, axis=1, keepdims=True) + 1e-6) * gain[...]
    n16 = jnp.concatenate([nf[:, :1024], nf[:, 1024:]], axis=0).astype(BF16)
    for k in range(NX):
        nsend[k] = n16[:, k * 256:(k + 1) * 256]
    nq[x, zhi, core] = nsend[x]
    wq[zlo, y] = wblk[...]
    lane = lax.broadcasted_iota(jnp.int32, (8, 128), 1)
    twice = jnp.broadcast_to(jnp.concatenate([idrow[...], idrow[...]], axis=1), (8, 128))
    idbuf[z] = jnp.where(lane // 64 == zlo, twice, 0)
    s_f = src[...].astype(F32)
    s_scale = lax.rsqrt(jnp.sum(s_f * s_f, axis=1, keepdims=True) + 1e-6)
    s_unit = (s_f * s_scale).astype(BF16)
    sbuf[0, z] = s_unit[:, :512]
    sbuf[1, z] = s_unit[:, 512:]

    pl.semaphore_wait(barrier, len(peers))

    started = []

    def cp(a, c, device):
        i = len(started)
        copy = pltpu.make_async_remote_copy(
            src_ref=a, dst_ref=c, send_sem=send_sem.at[i], recv_sem=recv_sem.at[i],
            device_id=device, device_id_type=MESH,
        )
        copy.start()
        started.append(copy)
        return copy

    def arrived(copies):
        for copy in copies:
            copy.wait_recv()

    def over_x(src_of, dst_of):
        return [cp(src_of(xd(d)), dst_of(d), dev(x=xd(d))) for d in FAR_X]

    def over_y(src_of, dst_of):
        return [cp(src_of(yd(d)), dst_of(d), dev(y=yd(d))) for d in FAR_Y]

    def over_zy(src_of, dst_of):
        return [
            cp(src_of(f, yd(d)), dst_of(NY * f + d), dev(y=yd(d), z=zp if f else z))
            for d in FAR_Y + (0,) for f in (1, 0) if f or d
        ]

    XZ = [(d, e) for e in (4, 2, 6, 0) for d in FAR_X + (0,)]
    own_w = wq.at[zlo, y]
    w1 = over_zy(lambda f, t: own_w, lambda i: own_w)
    c_n = [
        cp(nsend.at[xd(d)], nq.at[x, zhi, core], dev(x=xd(d), z=zd(e)))
        for d, e in XZ if d or e
    ]

    def hop(block, rows, step):
        ref = sbuf.at[:, block, rows]
        return cp(ref, ref, dev(z=zd(step)))

    every, low, high = pl.ds(0, 64), pl.ds(0, 32), pl.ds(32, 32)
    s_up, s_down = hop(z, every, 1), hop(z, every, 7)
    c_id = [cp(idbuf.at[z], idbuf.at[z], dev(z=zd(d))) for d in range(1, NZ)]

    arrived(c_n)
    c_ns = cp(nq.at[:, :, core], nq.at[:, :, core], dev(core=1 - core))
    arrived(w1)
    c_ns.wait_recv()

    halves = jnp.concatenate([wq[0].reshape(256, 128), wq[1].reshape(256, 128)], axis=1)
    both = dot(nq[...].reshape(512, 256), halves).reshape(32, 16, 256)
    rpart[...] = (both[:, 0:8, :128] + both[:, 8:16, 128:]).reshape(4, 4, 16, 128).astype(BF16)
    c_r = [
        cp(
            rpart.at[xd(d), zd(e) // 2], rbuf.at[x, p],
            dev(x=xd(d), z=zd(e), core=1 - core if flip else core),
        )
        for d, e in XZ for flip in (1, 0) if d or e or flip
    ]
    rbuf[x, p] = rpart[x, zhi]
    s_up.wait_recv()
    s_down.wait_recv()
    s_up, s_down = hop(zd(7), every, 1), hop(zd(1), every, 7)
    nt_buf[...] = nq[...].reshape(512, 256).T
    arrived(c_r)

    raw = jnp.sum(rbuf[...].astype(F32), axis=0).astype(BF16)
    raw_f = jnp.concatenate([raw[k] for k in range(8)], axis=1).astype(F32)
    g_scale = lax.rsqrt(jnp.sum(raw_f * raw_f, axis=1, keepdims=True) + 1e-6)
    g_unit = (raw_f * g_scale).astype(BF16)
    gown[0] = g_unit[:, :512]
    gown[1] = g_unit[:, 512:]
    gbuf[core, x, y] = gown[core]
    ga, gb = pl.ds(0, 128), pl.ds(128, 384)
    g1a = over_x(lambda t: gbuf.at[core, x, y, :, ga], lambda d: gbuf.at[core, x, y, :, ga])
    g1b = over_y(lambda t: gbuf.at[core, x, y, :, gb], lambda d: gbuf.at[core, x, y, :, gb])
    s_up.wait_recv()
    s_down.wait_recv()
    s_up, s_down = hop(zd(6), every, 1), hop(zd(2), every, 7)
    arrived(g1a)
    g2a = over_y(lambda t: gbuf.at[core, :, y, :, ga], lambda d: gbuf.at[core, :, y, :, ga])
    arrived(g1b)
    mine = gbuf.at[core, x, :, :, gb]
    g2b = {d: cp(mine, mine, dev(x=xd(d))) for d in FAR_X}
    s_up.wait_recv()
    s_down.wait_recv()
    s_up, s_down = hop(zd(5), low, 1), hop(zd(3), high, 7)
    arrived(g2a)

    sibling = dev(core=1 - core)
    c_g, c_u, u1b = {}, {}, []

    def share(d):
        if d:
            g2b[NX - d].wait_recv()
        block = gbuf.at[core, xd(d)]
        c_g[d] = cp(block, block, sibling)

    def weigh(pair):
        nt = ((1,), (1,))
        ks = [xd(d) for d in pair]
        for d in pair:
            c_g[d].wait_recv()
        g0, g1 = (
            jnp.concatenate([gbuf[h, k].reshape(128, 512) for k in ks], axis=0) for h in (0, 1)
        )
        sim = dot(g0, sbuf[0].reshape(512, 512), nt) + dot(g1, sbuf[1].reshape(512, 512), nt)
        logits = scale * sim + offset
        goal = jnp.concatenate(
            [(zlo * 32 + k * 8 + row // 16) * 64 + zhi * 16 + lax.rem(row, 16) for k in ks], axis=0
        )
        sign = jnp.where(goal == ids, 1.0, -1.0).astype(F32)
        weight = (-scale * sign / (1.0 + jnp.exp(sign * logits))).astype(BF16)
        for i, k in enumerate(ks):
            pt[pl.ds(pl.multiple_of(k * 128, 128), 128), :] = weight[i * 128:(i + 1) * 128]
        give = dot(weight, sbuf[1 - core].reshape(512, 512)).astype(BF16)
        for i, (d, k) in enumerate(zip(pair, ks)):
            usend[k] = give[i * 128:(i + 1) * 128].reshape(8, 16, 512)
            c_u[d] = cp(usend.at[k], urecv.at[k], sibling)
        keep = dot(weight, sbuf[core].reshape(512, 512))
        for i, k in enumerate(ks):
            uown[k] = keep[i * 128:(i + 1) * 128].reshape(8, 16, 512)

    def pass_on(d):
        k = xd(d)
        c_u[d].wait_recv()
        ub[k] = (uown[k] + urecv[k].astype(F32)).astype(BF16)
        if d:
            u1b.append(cp(ub.at[k, :, :, gb], ub1.at[d - 1], dev(x=k)))

    share(0)
    scale, offset = sharp[0], shift[0]
    row = lax.broadcasted_iota(jnp.int32, (128, 1), 0)
    arrived(c_id)
    ids = jnp.concatenate(
        [idbuf[2 * q, 0:1] + idbuf[2 * q + 1, 0:1] for q in range(4)], axis=1
    )
    s_up.wait_recv()
    s_down.wait_recv()
    share(1)
    weigh((0, 1))
    share(3)
    share(2)
    pass_on(1)
    pass_on(0)
    weigh((3, 2))
    pass_on(2)
    pass_on(3)
    u1a = over_y(lambda t: ub.at[:, t, :, ga], lambda d: ua1.at[d - 1])

    for q in range(4):
        lhs = pt[:, q * 128:(q + 1) * 128]
        for h in range(2):
            part = dot(lhs, gbuf[h].reshape(512, 512), ((0,), (0,)))
            spbuf[2 * q:2 * q + 2, h] = part.reshape(2, 64, 512).astype(BF16)

    low32, high32 = pl.ds(0, 32), pl.ds(32, 32)
    r_up = cp(spbuf.at[zd(4), :, low32], shalf.at[0], dev(z=zd(1)))
    r_down = cp(spbuf.at[zd(4), :, high32], shalf.at[1], dev(z=zd(7)))

    def relay(step, r_up, r_down):
        r_up.wait_recv()
        r_down.wait_recv()
        up, down = zd(4 - step), zd(4 + step)
        if step == 1:
            spbuf[up, :, 0:32] = (spbuf[up, :, 0:32].astype(F32) + shalf[0].astype(F32)).astype(BF16)
            spbuf[down, :, 32:64] = (spbuf[down, :, 32:64].astype(F32) + shalf[1].astype(F32)).astype(BF16)
        else:
            spbuf[up] = (spbuf[up].astype(F32) + srecv[step - 2, 0].astype(F32)).astype(BF16)
            spbuf[down] = (spbuf[down].astype(F32) + srecv[step - 2, 1].astype(F32)).astype(BF16)
        return (
            cp(spbuf.at[up], srecv.at[step - 1, 0], dev(z=zd(1))),
            cp(spbuf.at[down], srecv.at[step - 1, 1], dev(z=zd(7))),
        )

    arrived(u1a)
    ta[...] = (ub[:, y, :, 0:128].astype(F32) + jnp.sum(ua1[...].astype(F32), axis=0)).astype(BF16)
    u2a = over_x(lambda t: ta.at[t], lambda d: ua2.at[d - 1])
    arrived(u1b)
    tb[...] = (ub[x, :, :, 128:512].astype(F32) + jnp.sum(ub1[...].astype(F32), axis=0)).astype(BF16)
    u2b = over_y(lambda t: tb.at[t], lambda d: ub2.at[d - 1])
    r_up, r_down = relay(1, r_up, r_down)
    arrived(u2a)
    xbuf[core, :, 0:128] = ta[x].astype(F32) + jnp.sum(ua2[...].astype(F32), axis=0)
    arrived(u2b)
    xbuf[core, :, 128:512] = tb[y].astype(F32) + jnp.sum(ub2[...].astype(F32), axis=0)
    c_x = cp(xbuf.at[core], xbuf.at[core], dev(core=1 - core))
    r_up, r_down = relay(2, r_up, r_down)
    c_x.wait_recv()

    u = jnp.concatenate([xbuf[0], xbuf[1]], axis=1)
    g_f = raw_f * g_scale
    inner = jnp.sum(g_f * u, axis=1, keepdims=True)
    raw_grad = (g_scale * (u - g_f * inner)).astype(BF16)
    for k in range(8):
        rgb[k] = raw_grad[:, k * 128:(k + 1) * 128]
    rgr[x, zhi] = rgb[p]
    c_rg = [
        cp(rgb.at[(zd(e) // 2) * 2 + core], rgr.at[x, zhi], dev(x=xd(d), z=zd(e)))
        for d, e in XZ if d or e
    ]
    r_up, r_down = relay(3, r_up, r_down)
    arrived(c_rg)
    rg = rgr[...].astype(F32).reshape(32, 8, 128)
    zero = jnp.zeros((32, 8, 128), F32)
    rg_top = jnp.concatenate([rg, zero], axis=1).reshape(512, 128).astype(BF16)
    rg_bottom = jnp.concatenate([zero, rg], axis=1).reshape(512, 128).astype(BF16)
    part = dot(nt_buf[...], jnp.concatenate([rg_top, rg_bottom], axis=1)).astype(BF16)
    hq[0] = part[:, :128].reshape(8, 32, 128)
    hq[1] = part[:, 128:].reshape(8, 32, 128)
    c_h = over_zy(lambda f, t: hq.at[1 - zlo if f else zlo, t], lambda i: hsum.at[i])
    hsum[0] = hq[zlo, y]

    r_up.wait_recv()
    r_down.wait_recv()
    su_f = s_f * s_scale
    sums = spbuf[z].astype(F32) + srecv[2, 0].astype(F32) + srecv[2, 1].astype(F32)
    usg = jnp.concatenate([sums[0], sums[1]], axis=1)
    inner_s = jnp.sum(su_f * usg, axis=1, keepdims=True)
    sg_out[...] = (s_scale * (usg - su_f * inner_s)).astype(BF16)

    arrived(c_h)
    hg_out[...] = jnp.sum(hsum[...].astype(F32), axis=0)
    for copy in started:
        copy.wait_send()


def body(features, gain, weights, states, ids, sharpness, offset):
    vmem = pl.BlockSpec(memory_space=pltpu.VMEM)
    hbm = pl.BlockSpec(memory_space=pltpu.HBM)
    smem = pl.BlockSpec(memory_space=pltpu.SMEM)
    V = pltpu.VMEM
    return pl.pallas_call(
        kernel,
        out_shape=(
            jax.ShapeDtypeStruct((64, 1024), BF16),
            jax.ShapeDtypeStruct((32, 128), F32),
        ),
        in_specs=[hbm] * 5 + [smem] * 2,
        out_specs=(vmem, vmem),
        scratch_shapes=[
            V((8, 2048), BF16),
            V((1, 2048), F32),
            V((32, 128), BF16),
            V((64, 1024), BF16),
            V((1, 64), jnp.int32),
            V((4, 16, 256), BF16),
            V((4, 4, 2, 16, 256), BF16),
            V((2, 8, 32, 128), BF16),
            V((4, 4, 16, 128), BF16),
            V((4, 8, 16, 128), BF16),
            V((2, 16, 512), BF16),
            V((2, 4, 8, 16, 512), BF16),
            V((2, 8, 64, 512), BF16),
            V((8, 8, 128), jnp.int32),
            V((512, 512), BF16),
            V((4, 8, 16, 512), F32),
            V((4, 8, 16, 512), BF16),
            V((4, 8, 16, 512), BF16),
            V((4, 8, 16, 512), BF16),
            V((7, 4, 16, 128), BF16),
            V((3, 8, 16, 384), BF16),
            V((4, 16, 128), BF16),
            V((8, 16, 384), BF16),
            V((3, 16, 128), BF16),
            V((7, 16, 384), BF16),
            V((2, 16, 512), F32),
            V((8, 16, 128), BF16),
            V((4, 4, 16, 128), BF16),
            V((256, 512), BF16),
            V((2, 8, 32, 128), BF16),
            V((16, 32, 128), BF16),
            V((8, 2, 64, 512), BF16),
            V((2, 2, 32, 512), BF16),
            V((3, 2, 2, 64, 512), BF16),
            pltpu.SemaphoreType.DMA((N_SEM,)),
            pltpu.SemaphoreType.DMA((N_SEM,)),
            pltpu.SemaphoreType.DMA((5,)),
        ],
        compiler_params=pltpu.CompilerParams(
            collective_id=0, has_side_effects=True, vmem_limit_bytes=63 * 2**20
        ),
    )(features, gain.reshape(1, 2048), weights, states, ids.reshape(1, 64), sharpness, offset)


def solution(mesh):
    in_specs = (
        P(("batch", "param"), None),
        P(),
        P("batch", "param"),
        P(("batch", "param"), None),
        P(("batch", "param")),
        P(),
        P(),
    )
    out_specs = (P(("batch", "param"), None), P("batch", "param"))
    return jax.shard_map(body, mesh=mesh, in_specs=in_specs, out_specs=out_specs, check_vma=False)
```

time: 88.3 us -> 82.8 us (0.938)
  the two profiles are of different devices: /device:TPU:1 before, /device:TPU:8 now
where the time goes in v3:
time: 82.8 us; the launch traced here: 82.6 us
  Pallas kernels  78.5 us (95%)
  local copies, waits for them, and re-layouts  2.18 us (3%)
  between operations  1.94 us (2%)
    pallas_call x1, Pallas kernels, body(): pl.pallas_call(kernel, out_shape=(jax.ShapeDtypeStruct((64, 1024), BF16),...  78.5 us
    unnamed x4, local copies, waits for them, and re-layouts  2.18 us

profile of v3, /device:TPU:8, one launch (start us, length us, event | category | flops | bytes accessed | tf_op | source)
XLA Modules:
  0.0 82.6 jit_solution(10544330239130762567)
XLA Ops:
  1.9 78.5 %shard_map.86 = (bf16[64,1024]{1,0:T(8,128)(2,1)}, f32[32,128]{1,0:T(8,128)}) custom-call(bf16[8,2048]{1,0:T(8,128)(2,1)} %feat_in.1, f32[1,2048]{1,0:T(1,128)} %bitcast.2, bf16[32,128]{1,0:T(8,128)(2,1)} %wblk_in.1, bf16[64,1024]{1,0:T(8,128)(2,1)} %src_in.1, s32[1,64]{1,0:T(1,128)} %bitcast.3, f32[1]{0:T(128)S(6)} %copy.11.sharp, f32[1]{0:T(128)S(6)} %copy.12.shift), custom_call_target="tpu_custom_call" | custom-call | tf_op jit(solution)/shard_map/pallas_call | solution.py:321
  80.4 0.0 copy-start
  80.4 1.6 %copy.13 = bf16[64,1024]{1,0:T(8,128)(2,1)} copy(bf16[64,1024]{1,0:T(8,128)(2,1)} %get-tuple-element.4) | data formatting | bytes 262144
  82.0 0.0 copy-done
  82.0 0.6 copy.14
Async XLA Ops:
  80.4 1.6 %copy-start = (f32[32,128]{1,0:T(8,128)S(1)}, f32[32,128]{1,0:T(8,128)}, u32[]{:S(2)}) copy-start(f32[32,128]{1,0:T(8,128)} %get-tuple-element.5) | copy-start | bytes 49156

commit v4 on v3

--- a/solution.py
+++ b/solution.py
@@ -66,7 +66,7 @@
     for peer in peers:
         pl.semaphore_signal(barrier, inc=1, device_id=peer, device_id_type=MESH)
 
-    for load in loads:
+    for load in loads[:3]:
         load.wait()
     f = feat[...].astype(F32)
     nf = f * lax.rsqrt(jnp.mean(f * f, axis=1, keepdims=True) + 1e-6) * gain[...]
@@ -75,15 +75,6 @@
         nsend[k] = n16[:, k * 256:(k + 1) * 256]
     nq[x, zhi, core] = nsend[x]
     wq[zlo, y] = wblk[...]
-    lane = lax.broadcasted_iota(jnp.int32, (8, 128), 1)
-    twice = jnp.broadcast_to(jnp.concatenate([idrow[...], idrow[...]], axis=1), (8, 128))
-    idbuf[z] = jnp.where(lane // 64 == zlo, twice, 0)
-    s_f = src[...].astype(F32)
-    s_scale = lax.rsqrt(jnp.sum(s_f * s_f, axis=1, keepdims=True) + 1e-6)
-    s_unit = (s_f * s_scale).astype(BF16)
-    sbuf[0, z] = s_unit[:, :512]
-    sbuf[1, z] = s_unit[:, 512:]
-
     pl.semaphore_wait(barrier, len(peers))
 
     started = []
@@ -121,6 +112,17 @@
         cp(nsend.at[xd(d)], nq.at[x, zhi, core], dev(x=xd(d), z=zd(e)))
         for d, e in XZ if d or e
     ]
+
+    for load in loads[3:]:
+        load.wait()
+    lane = lax.broadcasted_iota(jnp.int32, (8, 128), 1)
+    twice = jnp.broadcast_to(jnp.concatenate([idrow[...], idrow[...]], axis=1), (8, 128))
+    idbuf[z] = jnp.where(lane // 64 == zlo, twice, 0)
+    s_f = src[...].astype(F32)
+    s_scale = lax.rsqrt(jnp.sum(s_f * s_f, axis=1, keepdims=True) + 1e-6)
+    s_unit = (s_f * s_scale).astype(BF16)
+    sbuf[0, z] = s_unit[:, :512]
+    sbuf[1, z] = s_unit[:, 512:]
 
     def hop(block, rows, step):
         ref = sbuf.at[:, block, rows]
@@ -184,30 +186,20 @@
         block = gbuf.at[core, xd(d)]
         c_g[d] = cp(block, block, sibling)
 
-    def weigh(pair):
+    def weigh(d):
+        k = xd(d)
+        c_g[d].wait_recv()
         nt = ((1,), (1,))
-        ks = [xd(d) for d in pair]
-        for d in pair:
-            c_g[d].wait_recv()
-        g0, g1 = (
-            jnp.concatenate([gbuf[h, k].reshape(128, 512) for k in ks], axis=0) for h in (0, 1)
-        )
-        sim = dot(g0, sbuf[0].reshape(512, 512), nt) + dot(g1, sbuf[1].reshape(512, 512), nt)
+        sim = dot(gbuf[0, k].reshape(128, 512), sbuf[0].reshape(512, 512), nt)
+        sim += dot(gbuf[1, k].reshape(128, 512), sbuf[1].reshape(512, 512), nt)
         logits = scale * sim + offset
-        goal = jnp.concatenate(
-            [(zlo * 32 + k * 8 + row // 16) * 64 + zhi * 16 + lax.rem(row, 16) for k in ks], axis=0
-        )
+        goal = (zlo * 32 + k * 8 + row // 16) * 64 + zhi * 16 + lax.rem(row, 16)
         sign = jnp.where(goal == ids, 1.0, -1.0).astype(F32)
         weight = (-scale * sign / (1.0 + jnp.exp(sign * logits))).astype(BF16)
-        for i, k in enumerate(ks):
-            pt[pl.ds(pl.multiple_of(k * 128, 128), 128), :] = weight[i * 128:(i + 1) * 128]
-        give = dot(weight, sbuf[1 - core].reshape(512, 512)).astype(BF16)
-        for i, (d, k) in enumerate(zip(pair, ks)):
-            usend[k] = give[i * 128:(i + 1) * 128].reshape(8, 16, 512)
-            c_u[d] = cp(usend.at[k], urecv.at[k], sibling)
-        keep = dot(weight, sbuf[core].reshape(512, 512))
-        for i, k in enumerate(ks):
-            uown[k] = keep[i * 128:(i + 1) * 128].reshape(8, 16, 512)
+        pt[pl.ds(pl.multiple_of(k * 128, 128), 128), :] = weight
+        usend[k] = dot(weight, sbuf[1 - core].reshape(512, 512)).reshape(8, 16, 512).astype(BF16)
+        c_u[d] = cp(usend.at[k], urecv.at[k], sibling)
+        uown[k] = dot(weight, sbuf[core].reshape(512, 512)).reshape(8, 16, 512)
 
     def pass_on(d):
         k = xd(d)
@@ -226,14 +218,16 @@
     s_up.wait_recv()
     s_down.wait_recv()
     share(1)
-    weigh((0, 1))
+    weigh(0)
     share(3)
+    weigh(1)
+    pass_on(0)
     share(2)
+    weigh(3)
     pass_on(1)
-    pass_on(0)
-    weigh((3, 2))
+    weigh(2)
+    pass_on(3)
     pass_on(2)
-    pass_on(3)
     u1a = over_y(lambda t: ub.at[:, t, :, ga], lambda d: ua1.at[d - 1])
 
     for q in range(4):
@@ -273,7 +267,6 @@
     arrived(u2b)
     xbuf[core, :, 128:512] = tb[y].astype(F32) + jnp.sum(ub2[...].astype(F32), axis=0)
     c_x = cp(xbuf.at[core], xbuf.at[core], dev(core=1 - core))
-    r_up, r_down = relay(2, r_up, r_down)
     c_x.wait_recv()
 
     u = jnp.concatenate([xbuf[0], xbuf[1]], axis=1)
@@ -287,7 +280,7 @@
         cp(rgb.at[(zd(e) // 2) * 2 + core], rgr.at[x, zhi], dev(x=xd(d), z=zd(e)))
         for d, e in XZ if d or e
     ]
-    r_up, r_down = relay(3, r_up, r_down)
+    r_up, r_down = relay(2, r_up, r_down)
     arrived(c_rg)
     rg = rgr[...].astype(F32).reshape(32, 8, 128)
     zero = jnp.zeros((32, 8, 128), F32)
@@ -298,6 +291,7 @@
     hq[1] = part[:, 128:].reshape(8, 32, 128)
     c_h = over_zy(lambda f, t: hq.at[1 - zlo if f else zlo, t], lambda i: hsum.at[i])
     hsum[0] = hq[zlo, y]
+    r_up, r_down = relay(3, r_up, r_down)
 
     r_up.wait_recv()
     r_down.wait_recv()
@@ -313,12 +307,17 @@
         copy.wait_send()
 
 
+def copy_out(sg_in, hg_in, sg_out, hg_out):
+    sg_out[...] = sg_in[...]
+    hg_out[...] = hg_in[...]
+
+
 def body(features, gain, weights, states, ids, sharpness, offset):
     vmem = pl.BlockSpec(memory_space=pltpu.VMEM)
     hbm = pl.BlockSpec(memory_space=pltpu.HBM)
     smem = pl.BlockSpec(memory_space=pltpu.SMEM)
     V = pltpu.VMEM
-    return pl.pallas_call(
+    sg, hg = pl.pallas_call(
         kernel,
         out_shape=(
             jax.ShapeDtypeStruct((64, 1024), BF16),
@@ -369,6 +368,15 @@
             collective_id=0, has_side_effects=True, vmem_limit_bytes=63 * 2**20
         ),
     )(features, gain.reshape(1, 2048), weights, states, ids.reshape(1, 64), sharpness, offset)
+    return pl.pallas_call(
+        copy_out,
+        out_shape=(
+            jax.ShapeDtypeStruct((64, 1024), BF16),
+            jax.ShapeDtypeStruct((32, 128), F32),
+        ),
+        in_specs=[vmem] * 2,
+        out_specs=(vmem, vmem),
+    )(sg, hg)
 
 
 def solution(mesh):

time: 82.8 us -> 80.3 us (0.970)
  the two profiles are of different devices: /device:TPU:8 before, /device:TPU:1 now
where the time goes in v4:
time: 80.3 us; the launch traced here: 80.2 us
  Pallas kernels  78.2 us (97%)
  between operations  1.93 us (2%)
    pallas_call x1, Pallas kernels, body(): pl.pallas_call(kernel, out_shape=(jax.ShapeDtypeStruct((64, 1024), BF16),...  76.6 us

profile of v4, /device:TPU:1, one launch (start us, length us, event | category | flops | bytes accessed | tf_op | source)
XLA Modules:
  0.0 80.2 jit_solution(16581086878518486730)
XLA Ops:
  1.9 76.6 %shard_map.86 = (bf16[64,1024]{1,0:T(8,128)(2,1)}, f32[32,128]{1,0:T(8,128)}) custom-call(bf16[8,2048]{1,0:T(8,128)(2,1)} %feat_in.1, f32[1,2048]{1,0:T(1,128)} %bitcast.2, bf16[32,128]{1,0:T(8,128)(2,1)} %wblk_in.1, bf16[64,1024]{1,0:T(8,128)(2,1)} %src_in.1, s32[1,64]{1,0:T(1,128)} %bitcast.3, f32[1]{0:T(128)S(6)} %copy.9.sharp, f32[1]{0:T(128)S(6)} %copy.10.shift), custom_call_target="tpu_custom_call" | custom-call | tf_op jit(solution)/shard_map/pallas_call | solution.py:320
  78.6 1.6 %shard_map.87 = (bf16[64,1024]{1,0:T(8,128)(2,1)}, f32[32,128]{1,0:T(8,128)}) custom-call(bf16[64,1024]{1,0:T(8,128)(2,1)} %get-tuple-element.4.sg_in, f32[32,128]{1,0:T(8,128)} %get-tuple-element.5.hg_in), custom_call_target="tpu_custom_call" | custom-call | tf_op jit(solution)/shard_map/pallas_call | solution.py:371

commit v5 on v4

--- a/solution.py
+++ b/solution.py
@@ -48,6 +48,15 @@
     def zd(d):
         return lax.rem(z + d, NZ)
 
+    peers = [dev(x=xd(d), z=zd(e), core=1 - core) for e in (4, 2, 6, 0) for d in (2, 1, 3, 0)]
+    peers += [dev(x=xd(d), z=zd(e)) for e in (4, 2, 6, 0) for d in (2, 1, 3)]
+    peers += [dev(y=yd(d), z=zp) for d in FAR_Y]
+    peers += [dev(y=yd(d)) for d in FAR_Y]
+    peers += [dev(z=zd(d)) for d in FAR_Y]
+    barrier = pltpu.get_barrier_semaphore()
+    for peer in peers:
+        pl.semaphore_signal(barrier, inc=1, device_id=peer, device_id_type=MESH)
+
     loads = [
         pltpu.make_async_copy(a, c, in_sem.at[i])
         for i, (a, c) in enumerate(
@@ -56,15 +65,6 @@
     ]
     for load in loads:
         load.start()
-
-    peers = [dev(y=yd(d)) for d in range(1, NY)]
-    peers += [dev(y=yd(d), z=zp) for d in range(1, NY)]
-    peers += [dev(z=zd(d)) for d in range(1, NZ)]
-    peers += [dev(x=xd(d), z=zd(e)) for d in (1, 2, 3) for e in (0, 2, 4, 6)]
-    peers += [dev(x=xd(d), z=zd(e), core=1 - core) for d in (0, 1, 2, 3) for e in (0, 2, 4, 6)]
-    barrier = pltpu.get_barrier_semaphore()
-    for peer in peers:
-        pl.semaphore_signal(barrier, inc=1, device_id=peer, device_id_type=MESH)
 
     for load in loads[:3]:
         load.wait()
@@ -107,11 +107,11 @@
 
     XZ = [(d, e) for e in (4, 2, 6, 0) for d in FAR_X + (0,)]
     own_w = wq.at[zlo, y]
-    w1 = over_zy(lambda f, t: own_w, lambda i: own_w)
     c_n = [
         cp(nsend.at[xd(d)], nq.at[x, zhi, core], dev(x=xd(d), z=zd(e)))
         for d, e in XZ if d or e
     ]
+    w1 = over_zy(lambda f, t: own_w, lambda i: own_w)
 
     for load in loads[3:]:
         load.wait()

time: 80.3 us -> 79.9 us (level)
  no operation moved by 1% of the time
where the time goes in v5:
time: 79.9 us; the launch traced here: 79.7 us
  Pallas kernels  77.8 us (97%)
  between operations  1.93 us (2%)
    pallas_call x1, Pallas kernels, body(): pl.pallas_call(kernel, out_shape=(jax.ShapeDtypeStruct((64, 1024), BF16),...  76.2 us

profile of v5, /device:TPU:1, one launch (start us, length us, event | category | flops | bytes accessed | tf_op | source)
XLA Modules:
  0.0 79.7 jit_solution(7014927306126678473)
XLA Ops:
  1.9 76.2 %shard_map.86 = (bf16[64,1024]{1,0:T(8,128)(2,1)}, f32[32,128]{1,0:T(8,128)}) custom-call(bf16[8,2048]{1,0:T(8,128)(2,1)} %feat_in.1, f32[1,2048]{1,0:T(1,128)} %bitcast.2, bf16[32,128]{1,0:T(8,128)(2,1)} %wblk_in.1, bf16[64,1024]{1,0:T(8,128)(2,1)} %src_in.1, s32[1,64]{1,0:T(1,128)} %bitcast.3, f32[1]{0:T(128)S(6)} %copy.9.sharp, f32[1]{0:T(128)S(6)} %copy.10.shift), custom_call_target="tpu_custom_call" | custom-call | tf_op jit(solution)/shard_map/pallas_call | solution.py:320
  78.1 1.6 %shard_map.87 = (bf16[64,1024]{1,0:T(8,128)(2,1)}, f32[32,128]{1,0:T(8,128)}) custom-call(bf16[64,1024]{1,0:T(8,128)(2,1)} %get-tuple-element.4.sg_in, f32[32,128]{1,0:T(8,128)} %get-tuple-element.5.hg_in), custom_call_target="tpu_custom_call" | custom-call | tf_op jit(solution)/shard_map/pallas_call | solution.py:371
